TPU v7x, 1024 devices: a whole 4x4x32 slice. The times are simulated.
1024 devices in a mesh: tens: 32 (over z), mat: 8 (over y, core), rep: 4 (over x).
Axes of the slice: x: 4, y: 4, z: 32, core: 2. Of those that a mesh axis runs over, the one named last changes fastest.
Arguments:
- integrals: bfloat16 [512, 512, 512], P(('tens', 'rep')), may hold values from -6 to 6
- block_mask: int32 [512, 4, 4], P(('tens', 'rep')), may hold values 0 or 1
- green_occ: bfloat16 [512, 512], replicated, may hold values from -0.25 to 0.25
- green_virt: bfloat16 [512, 512], P(None, 'mat'), may hold values from -0.25 to 0.25
Outputs:
- polar: float32 [512, 512], P(('tens', 'rep'), 'mat')
All inputs are finite; a program needn't handle non-finite values. No bound on the sum of `block_mask` on one device may be relied on, other than what follows from the above.
Results may differ from a plain program's by a relative error of at most 0.0041.
Values may be sent and summed in bfloat16 or wider, within the bound.
No kernel may reach another device: no remote copies, remote signals or barrier semaphores. Data moves between devices by JAX's collectives and lax.ppermute only.
A program may use at most 32 MiB of HBM per device.

v0:
```python
import jax
import jax.numpy as jnp
from jax import lax
from jax.sharding import PartitionSpec as P


def shards(integrals, block_mask, green_occ, green_virt):
    aux_local = integrals.shape[0]
    ao_total = integrals.shape[1]
    blocks = block_mask.shape[1]
    width = ao_total // blocks
    cols = green_virt.shape[1]
    factor = block_mask.astype(integrals.dtype)[:, :, None, :, None]
    masked = (integrals.reshape(aux_local, blocks, width, blocks, width) * factor).reshape(
        aux_local, ao_total, ao_total
    )
    half = jnp.einsum("aml,ls->ams", masked, green_virt, preferred_element_type=jnp.float32).astype(
        jnp.bfloat16
    )
    dressed = jnp.einsum("mn,ams->ans", green_occ, half, preferred_element_type=jnp.float32).astype(
        jnp.bfloat16
    )
    col_start = lax.axis_index("mat") * cols
    local_pairs = lax.dynamic_slice_in_dim(masked, col_start, cols, 2)
    scale = jnp.float32(1.0 / ao_total)
    tens_count = lax.axis_size("tens")
    rep_count = lax.axis_size("rep")
    pair_total = ao_total * cols
    first = pair_total // rep_count
    step_dressed, step_pairs = (
        lax.all_to_all(
            dressed.reshape(aux_local, rep_count, first),
            "rep",
            split_axis=1,
            concat_axis=0,
            tiled=True,
        ),
        lax.all_to_all(
            local_pairs.reshape(aux_local, rep_count, first),
            "rep",
            split_axis=1,
            concat_axis=0,
            tiled=True,
        ),
    )
    second = first // tens_count
    wide_dressed, wide_pairs = (
        lax.all_to_all(
            step_dressed.reshape(aux_local * rep_count, tens_count, second),
            "tens",
            split_axis=1,
            concat_axis=0,
            tiled=True,
        ),
        lax.all_to_all(
            step_pairs.reshape(aux_local * rep_count, tens_count, second),
            "tens",
            split_axis=1,
            concat_axis=0,
            tiled=True,
        ),
    )
    flat_dressed = wide_dressed.reshape(aux_local * rep_count * tens_count, second)
    flat_pairs = wide_pairs.reshape(aux_local * rep_count * tens_count, second)
    partial_value = jnp.dot(flat_dressed, flat_pairs.T, preferred_element_type=jnp.float32) * scale
    own_rows = lax.psum_scatter(partial_value, ("tens", "rep"), scatter_dimension=0, tiled=True)
    return lax.psum_scatter(own_rows, "mat", scatter_dimension=1, tiled=True)


def solution(mesh):
    return jax.shard_map(
        shards,
        mesh=mesh,
        in_specs=(
            P(("tens", "rep"), None, None),
            P(("tens", "rep"), None, None),
            P(),
            P(None, "mat"),
        ),
        out_specs=P(("tens", "rep"), "mat"),
        check_vma=False,
    )
```

profile of v0, /device:TPU:1, one launch (start us, length us, event | category | flops | bytes accessed | tf_op | source)
XLA Modules:
  0.0 687.8 jit_solution(7212310571118890370)
XLA Ops:
  6.5 0.8 convert_element_type.12
  7.3 0.6 mul.20
  7.9 2.2 mul.21
  10.2 2.9 mul.22
  13.0 0.9 fusion
  14.0 0.3 copy.10
  14.3 0.4 reshape.26
  14.7 0.9 copy.11
  15.6 4.8 all-to-all-start
  20.4 0.2 constant_dynamic-slice_fusion.1
  20.6 0.4 reshape.29
  21.0 0.9 copy.13
  21.9 4.0 all-to-all-done
  26.0 3.4 all-to-all-start.2
  29.4 0.2 reshape.27
  29.6 0.9 copy.12
  30.4 4.5 all-to-all-done.2
  34.9 28.5 %all-to-all-start.1 = ((bf16[16,32,256]{2,0,1:T(8,128)(2,1)}), bf16[16,32,256]{2,0,1:T(8,128)(2,1)S(1)}, u32[]{:S(2)}, u32[]{:S(2)}) async-start(bf16[16,32,256]{2,0,1:T(8,128)(2,1)} %copy.12), calls=%async_computation.1 | async-start | bytes 524288 | tf_op jit(solution)/shard_map/all_to_all | solution.py:48
  63.4 0.0 all-reduce.3.cloned.1.call-start
  63.4 0.2 reshape.30
  63.6 0.2 copy.14
  63.7 37.5 %all-to-all-done.1 = bf16[16,32,256]{2,0,1:T(8,128)(2,1)S(1)} async-done(((bf16[16,32,256]{2,0,1:T(8,128)(2,1)}), bf16[16,32,256]{2,0,1:T(8,128)(2,1)S(1)}, u32[]{:S(2)}, u32[]{:S(2)}) %all-to-all-start.1) | async-done | bytes 262176 | tf_op jit(solution)/shard_map/all_to_all | solution.py:48
  101.2 43.4 %all_to_all.60 = bf16[16,32,256]{2,0,1:T(8,128)(2,1)S(1)} all-to-all(bf16[16,32,256]{2,0,1:T(8,128)(2,1)S(1)} %copy.14), channel_id=1, replica_groups=mesh['tens'=32,'mat'=8,'rep'=4] {'tens'}, dimensions={1} | all-to-all | bytes 524288 | tf_op jit(solution)/shard_map/all_to_all | solution.py:55
  144.6 1.4 convolution_multiply_fusion
  145.9 0.0 all-reduce.3.cloned.1.call-update
  145.9 0.0 reduce-scatter.4.cloned.1.call-start
  146.0 1.3 dynamic-slice
  147.9 469.7 %all-reduce.3.cloned.1.call-done = f32[512,512]{1,0:T(8,128)} async-done(((f32[512,512]{1,0:T(8,128)}), f32[512,512]{1,0:T(8,128)}) %all-reduce.3.cloned.1.call-update) | async-done | bytes 1048592
  617.6 0.7 constant_dynamic-slice_fusion
  618.3 0.9 copy.15
  619.2 60.3 %reduce-scatter.4.cloned.1.call-done = f32[64,4]{1,0:T(8,128)} async-done(((f32[512,4]{1,0:T(8,128)}), f32[64,4]{1,0:T(8,128)}) %reduce-scatter.4.cloned.1.call-update) | async-done | bytes 1040
  679.5 1.4 copy.16
  (5 shorter events, 0.0 us)
Async XLA Ops:
  6.5 6.5 copy-start
  10.2 2.9 copy-start.1
  15.6 10.4 %all-to-all-start = ((bf16[4,4,8192]{2,0,1:T(4,128)(2,1)}), bf16[4,4,8192]{2,0,1:T(4,128)(2,1)S(1)}, u32[]{:S(2)}, u32[]{:S(2)}) async-start(bf16[4,4,8192]{2,0,1:T(4,128)(2,1)} %copy.11), calls=%async_computation | async-start | bytes 524288 | tf_op jit(solution)/shard_map/all_to_all | solution.py:31
  26.0 8.9 %all-to-all-start.2 = ((bf16[4,4,8192]{2,0,1:T(4,128)(2,1)}), bf16[4,4,8192]{2,0,1:T(4,128)(2,1)S(1)}, u32[]{:S(2)}, u32[]{:S(2)}) async-start(bf16[4,4,8192]{2,0,1:T(4,128)(2,1)} %copy.13), calls=%async_computation.2 | async-start | bytes 524288 | tf_op jit(solution)/shard_map/all_to_all | solution.py:38
  34.9 66.3 %all-to-all-start.1 = ((bf16[16,32,256]{2,0,1:T(8,128)(2,1)}), bf16[16,32,256]{2,0,1:T(8,128)(2,1)S(1)}, u32[]{:S(2)}, u32[]{:S(2)}) async-start(bf16[16,32,256]{2,0,1:T(8,128)(2,1)} %copy.12), calls=%async_computation.1 | async-start | bytes 524288 | tf_op jit(solution)/shard_map/all_to_all | solution.py:48
  63.4 554.2 %all-reduce.3.cloned.1.call-start = ((), (), s32[]{:S(2)}) async-start(), calls=%async_computation.6 | async-start | bytes 2097152
  145.9 533.6 %reduce-scatter.4.cloned.1.call-start = ((), (), s32[]{:S(2)}) async-start(), calls=%async_computation.5 | async-start | bytes 294912
Sparse Core Ops, SparseCore 0:
  146.1 471.4 all-reduce.2
  621.3 58.1 reduce-scatter.3
where the time goes:
time: 688 us
  waiting for transfers between devices  576 us (84%)
  blocking collectives  43.4 us (6%)
  starting transfers between devices  36.8 us (5%)
  between operations  14.2 us (2%)
  local copies, waits for them, and re-layouts  11.6 us (2%)
    unnamed x4, waiting for transfers between devices  530 us
    all_to_all x1, blocking collectives, shards(): lax.all_to_all(step_pairs.reshape(aux_local * rep_count, tens_count, seco...  43.4 us
    all_to_all x1, waiting for transfers between devices, shards(): lax.all_to_all(step_dressed.reshape(aux_local * rep_count, tens_count, se...  37.5 us
    all_to_all x1, starting transfers between devices, shards(): lax.all_to_all(step_dressed.reshape(aux_local * rep_count, tens_count, se...  28.5 us
  transfers between devices with their start and end apart: 5, of which 5 were waited for; matrix products, arithmetic and copies ran while one was open for 1% of the time, Pallas kernels for 0%

commit v1 on v0

v1 whole, which is shorter than its diff:
```python
import jax
import jax.numpy as jnp
from jax import lax
from jax.experimental import pallas as pl
from jax.experimental.pallas import tpu as pltpu
from jax.sharding import PartitionSpec as P

BF = jnp.bfloat16
F32 = jnp.float32
NT = (((1,), (1,)), ((), ()))
LIMIT = pltpu.CompilerParams(vmem_limit_bytes=32 * 1024 * 1024)


def one_hot(rows, cols, column_of):
    row = lax.broadcasted_iota(jnp.int32, (rows, 1), 0)
    col = lax.broadcasted_iota(jnp.int32, (rows, cols), 1)
    return jnp.where(column_of(row) == col, 1.0, 0.0).astype(BF)


def dress_kernel(
    mask_hbm, virt_hbm, occ_hbm, slab_hbm, out_ref,
    mask_ref, left_ref, occ_ref, slab_ref, half_ref, rows_ref, sems,
):
    auxs, total, _ = slab_ref.shape
    blocks = mask_ref.shape[1]
    width = total // blocks
    cols = virt_hbm.shape[0]
    first = [
        pltpu.make_async_copy(mask_hbm, mask_ref, sems.at[0]),
        pltpu.make_async_copy(virt_hbm, left_ref.at[pl.ds(0, cols)], sems.at[1]),
    ]
    slabs = [
        pltpu.make_async_copy(slab_hbm.at[a], slab_ref.at[a], sems.at[3 + a]) for a in range(auxs)
    ]
    occ = pltpu.make_async_copy(occ_hbm, occ_ref, sems.at[2])
    for copy in first + slabs + [occ]:
        copy.start()

    start = lax.axis_index("mat") * cols
    left_ref[cols:, :] = one_hot(cols, total, lambda row: row + start)
    height = rows_ref.shape[0]
    kinds = height // cols
    order = one_hot(height, height, lambda row: (row % kinds) * cols + row // kinds)
    lane_block = lax.broadcasted_iota(jnp.int32, (1, total), 1) // width

    for copy in first:
        copy.wait()
    for a in range(auxs):
        slabs[a].wait()
        for b in range(0, blocks, 2):
            strips = []
            for row in (b, b + 1):
                kept = mask_ref[a, row : row + 1, :].astype(F32)
                factor = jnp.zeros((1, total), F32)
                for c in range(blocks):
                    factor = jnp.where(lane_block == c, kept[:, c : c + 1], factor)
                strips.append(slab_ref[a, row * width : (row + 1) * width, :] * factor.astype(BF))
            strip = jnp.concatenate(strips, axis=0)
            at = slice(b * width, (b + 2) * width)
            both = lax.dot_general(left_ref[...], strip, NT, preferred_element_type=F32).astype(BF)
            half_ref[a * cols : (a + 1) * cols, at] = both[:cols]
            rows_ref[(auxs + a) * cols : (auxs + a + 1) * cols, at] = both[cols:]
    occ.wait()
    rows_ref[: auxs * cols, :] = jnp.dot(
        half_ref[...], occ_ref[...], preferred_element_type=F32
    ).astype(BF)
    sorted_rows = jnp.dot(order, rows_ref[...], preferred_element_type=F32).astype(BF)
    parts, lanes = out_ref.shape[0], out_ref.shape[2]
    for h in range(parts):
        out_ref[h] = sorted_rows[:, h * lanes : (h + 1) * lanes]


def pair_kernel(tens_count, rep_count, folds, scale, got_ref, out_ref):
    height = got_ref.shape[0]
    kinds = height // (tens_count * rep_count)
    aux = kinds // 2
    total = height // 2
    per_rep = tens_count * aux

    low_count = aux // folds

    def dressed_row(row):
        r, rest = row // per_rep, row % per_rep
        high, rest = rest // (tens_count * low_count), rest % (tens_count * low_count)
        t, low = rest // low_count, rest % low_count
        return (t * rep_count + r) * kinds + high * low_count + low

    def masked_row(row):
        return (row // aux) * kinds + aux + row % aux

    got = got_ref[...]
    dressed = jnp.dot(
        one_hot(total, height, dressed_row), got, preferred_element_type=F32
    ).astype(BF)
    masked = jnp.dot(
        one_hot(total, height, masked_row), got, preferred_element_type=F32
    ).astype(BF)
    groups, cols, lanes = out_ref.shape
    for m in range(groups // rep_count):
        strip = lax.dot_general(
            masked[m * cols : (m + 1) * cols], dressed, NT, preferred_element_type=F32
        )
        strip = (strip * scale).astype(out_ref.dtype)
        for r in range(rep_count):
            out_ref[m * rep_count + r] = strip[:, r * lanes : (r + 1) * lanes]


def plane_kernel(got_ref, out_ref):
    total = got_ref[0].astype(F32)
    for k in range(1, got_ref.shape[0]):
        total = total + got_ref[k].astype(F32)
    rows = out_ref.shape[0]
    folds = total.shape[1] // rows
    out_ref[...] = jnp.concatenate(
        [total[:, h * rows : (h + 1) * rows].T for h in range(folds)], axis=1
    )


def own_kernel(got_ref, out_ref):
    total = got_ref[0]
    for k in range(1, got_ref.shape[0]):
        total = total + got_ref[k]
    low_count = total.shape[0]
    auxs, cols = out_ref.shape
    for h in range(auxs // low_count):
        out_ref[h * low_count : (h + 1) * low_count, :] = total[:, h * cols : (h + 1) * cols]


def shards(integrals, block_mask, green_occ, green_virt):
    auxs, total, _ = integrals.shape
    cols = green_virt.shape[1]
    tens_count = lax.axis_size("tens")
    rep_count = lax.axis_size("rep")
    mat_count = lax.axis_size("mat")
    owners = tens_count * rep_count
    kinds = 2 * auxs
    parts = owners // cols
    lanes = total // parts

    hbm = pl.BlockSpec(memory_space=pltpu.HBM)
    send = pl.pallas_call(
        dress_kernel,
        out_shape=jax.ShapeDtypeStruct((parts, cols * kinds, lanes), BF),
        in_specs=[hbm] * 4,
        scratch_shapes=[
            pltpu.VMEM(block_mask.shape, jnp.int32),
            pltpu.VMEM((2 * cols, total), BF),
            pltpu.VMEM((total, total), BF),
            pltpu.VMEM(integrals.shape, BF),
            pltpu.VMEM((auxs * cols, total), BF),
            pltpu.VMEM((kinds * cols, total), BF),
            pltpu.SemaphoreType.DMA((3 + auxs,)),
        ],
        compiler_params=pltpu.CompilerParams(vmem_limit_bytes=56 * 1024 * 1024),
        name="dress",
    )(block_mask, green_virt.T, green_occ, integrals)

    got = lax.all_to_all(
        send.reshape(owners, kinds, lanes), ("tens", "rep"), 0, 0, tiled=True
    )

    folds = min(auxs, max(1, 128 // cols))
    partial = pl.pallas_call(
        lambda *refs: pair_kernel(tens_count, rep_count, folds, 1.0 / total, *refs),
        out_shape=jax.ShapeDtypeStruct((mat_count * rep_count, cols, tens_count * auxs), F32),
        compiler_params=LIMIT,
        name="pair",
    )(got.reshape(owners * kinds, lanes))
    partial = lax.all_to_all(partial, ("mat", "rep"), 0, 0, tiled=True)

    rows = pl.pallas_call(
        plane_kernel,
        out_shape=jax.ShapeDtypeStruct((tens_count * auxs // folds, folds * cols), F32),
        compiler_params=LIMIT,
        name="plane_sum",
    )(partial)
    rows = rows.reshape(tens_count, auxs // folds, folds * cols)
    rows = lax.all_to_all(rows, "tens", 0, 0, tiled=True)
    return pl.pallas_call(
        own_kernel,
        out_shape=jax.ShapeDtypeStruct((auxs, cols), F32),
        compiler_params=LIMIT,
        name="own_sum",
    )(rows)


def solution(mesh):
    return jax.shard_map(
        shards,
        mesh=mesh,
        in_specs=(
            P(("tens", "rep"), None, None),
            P(("tens", "rep"), None, None),
            P(),
            P(None, "mat"),
        ),
        out_specs=P(("tens", "rep"), "mat"),
        check_vma=False,
    )
```

time: 688 us -> 153 us (0.22)
  waiting for transfers between devices: 576 us -> 0 us
  blocking collectives: 43.4 us -> 146 us
  starting transfers between devices: 36.8 us -> 0 us
  between operations: 14.2 us -> 0.02 us
  local copies, waits for them, and re-layouts: 11.6 us -> 0 us
    unnamed x4 -> x0, waiting for transfers between devices: 530 us -> none
    all_to_all x1 -> x3, blocking collectives: 43.4 us -> 146 us  [the longest x1 84.2 us: shards(): lax.all_to_all(send.reshape(owners, kinds, lanes), ('tens', 'rep'), 0, 0,...]
    all_to_all x3 -> x0, waiting for transfers between devices: 45.9 us -> none  [the longest x1 37.5 us: shards(): lax.all_to_all(step_dressed.reshape(aux_local * rep_count, tens_count, se...]
    all_to_all x3 -> x0, starting transfers between devices: 36.7 us -> none  [the longest x1 28.5 us: shards(): lax.all_to_all(step_dressed.reshape(aux_local * rep_count, tens_count, se...]
  transfers between devices with their start and end apart: 5 -> 0, of which waited for: 5 -> 0; matrix products, arithmetic and copies ran while one was open for 1% -> 0% of each run, Pallas kernels for 0% -> 0%
where the time goes in v1:
time: 153 us
  blocking collectives  146 us (95%)
  Pallas kernels  6.66 us (4%)
    all_to_all x1, blocking collectives, shards(): lax.all_to_all(send.reshape(owners, kinds, lanes), ('tens', 'rep'), 0, 0,...  84.2 us
    all_to_all x1, blocking collectives, shards(): partial = lax.all_to_all(partial, ('mat', 'rep'), 0, 0, tiled=True)  36.2 us
    all_to_all x1, blocking collectives, shards(): rows = lax.all_to_all(rows, 'tens', 0, 0, tiled=True)  25.4 us
    pallas_call x1, Pallas kernels, shards(): pl.pallas_call(dress_kernel, out_shape=jax.ShapeDtypeStruct((parts, cols...  4.23 us

profile of v1, /device:TPU:1, one launch (start us, length us, event | category | flops | bytes accessed | tf_op | source)
XLA Modules:
  0.0 152.5 jit_solution(2314054565294449268)
XLA Ops:
  0.0 4.2 %dress.1 = bf16[2,512,256]{2,1,0:T(8,128)(2,1)} custom-call(s32[4,4,4]{2,1,0:T(4,128)} %mask_hbm.1, bf16[64,512]{1,0:T(8,128)(2,1)} %bitcast.7, bf16[512,512]{1,0:T(8,128)(2,1)} %occ_hbm.1, bf16[4,512,512]{2,1,0:T(8,128)(2,1)} %slab_hbm.1), custom_call_target="tpu_custom_call" | custom-call | tf_op jit(solution)/shard_map/dress/pallas_call | solution.py:141
  4.2 84.2 %all_to_all.15 = bf16[128,8,256]{2,1,0:T(8,128)(2,1)S(1)} all-to-all(bf16[128,8,256]{2,1,0:T(8,128)(2,1)} %bitcast.6), channel_id=1, replica_groups=mesh['tens'=32,'mat'=8,'rep'=4] {'tens','rep'}, dimensions={0} | all-to-all | bytes 1048576 | tf_op jit(solution)/shard_map/all_to_all | solution.py:158
  88.4 1.5 pair.1
  89.9 36.2 %all_to_all.16.got_ref = f32[32,64,128]{2,1,0:T(8,128)S(1)} all-to-all(f32[32,64,128]{2,1,0:T(8,128)S(1)} %pair.1), channel_id=1, replica_groups=mesh['tens'=32,'mat'=8,'rep'=4] {'mat','rep'}, dimensions={0} | all-to-all | bytes 2097152 | tf_op jit(solution)/shard_map/all_to_all | solution.py:169
  126.2 0.3 plane_sum.1
  126.4 25.4 %all_to_all.17.got_ref = f32[32,2,128]{2,1,0:T(2,128)S(1)} all-to-all(f32[32,2,128]{2,1,0:T(2,128)S(1)} %bitcast.5), channel_id=1, replica_groups=mesh['tens'=32,'mat'=8,'rep'=4] {'tens'}, dimensions={0} | all-to-all | bytes 65536 | tf_op jit(solution)/shard_map/all_to_all | solution.py:178
  151.9 0.7 own_sum.1

commit v2 on v1

--- a/solution.py
+++ b/solution.py
@@ -162,7 +162,7 @@
     folds = min(auxs, max(1, 128 // cols))
     partial = pl.pallas_call(
         lambda *refs: pair_kernel(tens_count, rep_count, folds, 1.0 / total, *refs),
-        out_shape=jax.ShapeDtypeStruct((mat_count * rep_count, cols, tens_count * auxs), F32),
+        out_shape=jax.ShapeDtypeStruct((mat_count * rep_count, cols, tens_count * auxs), BF),
         compiler_params=LIMIT,
         name="pair",
     )(got.reshape(owners * kinds, lanes))

time: 153 us -> 148 us (0.967)
  blocking collectives: 146 us -> 141 us
    all_to_all x1, blocking collectives: 36.2 us -> 31.6 us  [shards(): partial = lax.all_to_all(partial, ('mat', 'rep'), 0, 0, tiled=True)]
where the time goes in v2:
time: 148 us
  blocking collectives  141 us (95%)
  Pallas kernels  6.68 us (5%)
    all_to_all x1, blocking collectives, shards(): lax.all_to_all(send.reshape(owners, kinds, lanes), ('tens', 'rep'), 0, 0,...  84.2 us
    all_to_all x1, blocking collectives, shards(): partial = lax.all_to_all(partial, ('mat', 'rep'), 0, 0, tiled=True)  31.6 us
    all_to_all x1, blocking collectives, shards(): rows = lax.all_to_all(rows, 'tens', 0, 0, tiled=True)  25.4 us
    pallas_call x1, Pallas kernels, shards(): pl.pallas_call(dress_kernel, out_shape=jax.ShapeDtypeStruct((parts, cols...  4.23 us

profile of v2, /device:TPU:1, one launch (start us, length us, event | category | flops | bytes accessed | tf_op | source)
XLA Modules:
  0.0 147.9 jit_solution(14671870433200575547)
XLA Ops:
  0.0 4.2 %dress.1 = bf16[2,512,256]{2,1,0:T(8,128)(2,1)} custom-call(s32[4,4,4]{2,1,0:T(4,128)} %mask_hbm.1, bf16[64,512]{1,0:T(8,128)(2,1)} %bitcast.7, bf16[512,512]{1,0:T(8,128)(2,1)} %occ_hbm.1, bf16[4,512,512]{2,1,0:T(8,128)(2,1)} %slab_hbm.1), custom_call_target="tpu_custom_call" | custom-call | tf_op jit(solution)/shard_map/dress/pallas_call | solution.py:141
  4.2 84.2 %all_to_all.15 = bf16[128,8,256]{2,1,0:T(8,128)(2,1)S(1)} all-to-all(bf16[128,8,256]{2,1,0:T(8,128)(2,1)} %bitcast.6), channel_id=1, replica_groups=mesh['tens'=32,'mat'=8,'rep'=4] {'tens','rep'}, dimensions={0} | all-to-all | bytes 1048576 | tf_op jit(solution)/shard_map/all_to_all | solution.py:158
  88.4 1.5 %pair.1 = bf16[32,64,128]{2,1,0:T(8,128)(2,1)S(1)} custom-call(bf16[1024,256]{1,0:T(8,128)(2,1)S(1)} %bitcast.4), custom_call_target="tpu_custom_call" | custom-call | tf_op jit(solution)/shard_map/pair/pallas_call | solution.py:163
  89.9 31.6 %all_to_all.16.got_ref = bf16[32,64,128]{2,1,0:T(8,128)(2,1)S(1)} all-to-all(bf16[32,64,128]{2,1,0:T(8,128)(2,1)S(1)} %pair.1), channel_id=1, replica_groups=mesh['tens'=32,'mat'=8,'rep'=4] {'mat','rep'}, dimensions={0} | all-to-all | bytes 1048576 | tf_op jit(solution)/shard_map/all_to_all | solution.py:169
  121.5 0.3 plane_sum.1
  121.8 25.4 %all_to_all.17.got_ref = f32[32,2,128]{2,1,0:T(2,128)S(1)} all-to-all(f32[32,2,128]{2,1,0:T(2,128)S(1)} %bitcast.5), channel_id=1, replica_groups=mesh['tens'=32,'mat'=8,'rep'=4] {'tens'}, dimensions={0} | all-to-all | bytes 65536 | tf_op jit(solution)/shard_map/all_to_all | solution.py:178
  147.2 0.7 own_sum.1

commit v3 on v2

--- a/solution.py
+++ b/solution.py
@@ -18,33 +18,34 @@
 
 
 def dress_kernel(
-    mask_hbm, virt_hbm, occ_hbm, slab_hbm, out_ref,
-    mask_ref, left_ref, occ_ref, slab_ref, half_ref, rows_ref, sems,
+    mask_hbm, virt_hbm, occ_hbm, slab_hbm, out_hbm,
+    mask_ref, left_ref, occ_ref, slab_ref, half_ref, rows_ref, out_ref, sems,
 ):
     auxs, total, _ = slab_ref.shape
     blocks = mask_ref.shape[1]
     width = total // blocks
     cols = virt_hbm.shape[0]
-    first = [
-        pltpu.make_async_copy(mask_hbm, mask_ref, sems.at[0]),
-        pltpu.make_async_copy(virt_hbm, left_ref.at[pl.ds(0, cols)], sems.at[1]),
-    ]
+    mask = pltpu.make_async_copy(mask_hbm, mask_ref, sems.at[0])
+    virt = pltpu.make_async_copy(virt_hbm, left_ref.at[pl.ds(0, cols)], sems.at[1])
+    occ = pltpu.make_async_copy(occ_hbm, occ_ref, sems.at[2])
     slabs = [
         pltpu.make_async_copy(slab_hbm.at[a], slab_ref.at[a], sems.at[3 + a]) for a in range(auxs)
     ]
-    occ = pltpu.make_async_copy(occ_hbm, occ_ref, sems.at[2])
-    for copy in first + slabs + [occ]:
+    for copy in [mask, virt] + slabs[:1] + [occ] + slabs[1:]:
         copy.start()
 
     start = lax.axis_index("mat") * cols
     left_ref[cols:, :] = one_hot(cols, total, lambda row: row + start)
-    height = rows_ref.shape[0]
-    kinds = height // cols
-    order = one_hot(height, height, lambda row: (row % kinds) * cols + row // kinds)
+    kinds = rows_ref.shape[0] // cols
+    band = min(cols, 32)
+    order = one_hot(
+        kinds * band, kinds * band, lambda row: (row % kinds) * band + row // kinds
+    )
     lane_block = lax.broadcasted_iota(jnp.int32, (1, total), 1) // width
 
-    for copy in first:
-        copy.wait()
+    mask.wait()
+    virt.wait()
+    done = 0
     for a in range(auxs):
         slabs[a].wait()
         for b in range(0, blocks, 2):
@@ -60,49 +61,83 @@
             both = lax.dot_general(left_ref[...], strip, NT, preferred_element_type=F32).astype(BF)
             half_ref[a * cols : (a + 1) * cols, at] = both[:cols]
             rows_ref[(auxs + a) * cols : (auxs + a + 1) * cols, at] = both[cols:]
-    occ.wait()
-    rows_ref[: auxs * cols, :] = jnp.dot(
-        half_ref[...], occ_ref[...], preferred_element_type=F32
-    ).astype(BF)
-    sorted_rows = jnp.dot(order, rows_ref[...], preferred_element_type=F32).astype(BF)
+        if a == 0:
+            occ.wait()
+        if a % 2 == 1 or a == auxs - 1:
+            at = slice(done * cols, (a + 1) * cols)
+            rows_ref[at, :] = jnp.dot(
+                half_ref[at, :], occ_ref[...], preferred_element_type=F32
+            ).astype(BF)
+            done = a + 1
+
     parts, lanes = out_ref.shape[0], out_ref.shape[2]
+    outs = []
     for h in range(parts):
-        out_ref[h] = sorted_rows[:, h * lanes : (h + 1) * lanes]
+        for g in range(cols // band):
+            rows = jnp.concatenate(
+                [
+                    rows_ref[
+                        j * cols + g * band : j * cols + (g + 1) * band,
+                        h * lanes : (h + 1) * lanes,
+                    ]
+                    for j in range(kinds)
+                ],
+                axis=0,
+            )
+            out_ref[h, g * kinds * band : (g + 1) * kinds * band, :] = jnp.dot(
+                order, rows, preferred_element_type=F32
+            ).astype(BF)
+        copy = pltpu.make_async_copy(out_ref.at[h], out_hbm.at[h], sems.at[3 + auxs + h])
+        copy.start()
+        outs.append(copy)
+    for copy in outs:
+        copy.wait()
 
 
 def pair_kernel(tens_count, rep_count, folds, scale, got_ref, out_ref):
     height = got_ref.shape[0]
     kinds = height // (tens_count * rep_count)
     aux = kinds // 2
-    total = height // 2
-    per_rep = tens_count * aux
-
     low_count = aux // folds
-
-    def dressed_row(row):
-        r, rest = row // per_rep, row % per_rep
-        high, rest = rest // (tens_count * low_count), rest % (tens_count * low_count)
+    near = min(tens_count, max(1, 256 // (rep_count * kinds)))
+    rows = near * rep_count * kinds
+    piece = near * low_count
+
+    def source_row(row):
+        r, rest = row // (near * aux), row % (near * aux)
+        high, rest = rest // piece, rest % piece
         t, low = rest // low_count, rest % low_count
-        return (t * rep_count + r) * kinds + high * low_count + low
-
-    def masked_row(row):
-        return (row // aux) * kinds + aux + row % aux
-
-    got = got_ref[...]
-    dressed = jnp.dot(
-        one_hot(total, height, dressed_row), got, preferred_element_type=F32
-    ).astype(BF)
-    masked = jnp.dot(
-        one_hot(total, height, masked_row), got, preferred_element_type=F32
-    ).astype(BF)
-    groups, cols, lanes = out_ref.shape
-    for m in range(groups // rep_count):
-        strip = lax.dot_general(
-            masked[m * cols : (m + 1) * cols], dressed, NT, preferred_element_type=F32
-        )
-        strip = (strip * scale).astype(out_ref.dtype)
-        for r in range(rep_count):
-            out_ref[m * rep_count + r] = strip[:, r * lanes : (r + 1) * lanes]
+        dressed = (t * rep_count + r) * kinds + high * low_count + low
+        back = row - rows // 2
+        masked = (back // aux) * kinds + aux + back % aux
+        return jnp.where(row < rows // 2, dressed, masked)
+
+    order = one_hot(rows, rows, source_row)
+    groups = [
+        jnp.dot(
+            order, got_ref[g * rows : (g + 1) * rows, :], preferred_element_type=F32
+        ).astype(BF)
+        for g in range(height // rows)
+    ]
+    dressed = jnp.concatenate(
+        [
+            group[(r * folds + high) * piece : (r * folds + high + 1) * piece]
+            for r in range(rep_count)
+            for high in range(folds)
+            for group in groups
+        ],
+        axis=0,
+    )
+    slots, cols, lanes = out_ref.shape
+    for g, group in enumerate(groups):
+        block = lax.dot_general(group[rows // 2 :], dressed, NT, preferred_element_type=F32)
+        block = (block * scale).astype(out_ref.dtype)
+        per = block.shape[0] // cols
+        for k in range(per):
+            for r in range(rep_count):
+                out_ref[(g * per + k) * rep_count + r] = block[
+                    k * cols : (k + 1) * cols, r * lanes : (r + 1) * lanes
+                ]
 
 
 def plane_kernel(got_ref, out_ref):
@@ -142,6 +177,7 @@
         dress_kernel,
         out_shape=jax.ShapeDtypeStruct((parts, cols * kinds, lanes), BF),
         in_specs=[hbm] * 4,
+        out_specs=hbm,
         scratch_shapes=[
             pltpu.VMEM(block_mask.shape, jnp.int32),
             pltpu.VMEM((2 * cols, total), BF),
@@ -149,7 +185,8 @@
             pltpu.VMEM(integrals.shape, BF),
             pltpu.VMEM((auxs * cols, total), BF),
             pltpu.VMEM((kinds * cols, total), BF),
-            pltpu.SemaphoreType.DMA((3 + auxs,)),
+            pltpu.VMEM((parts, cols * kinds, lanes), BF),
+            pltpu.SemaphoreType.DMA((3 + auxs + parts,)),
         ],
         compiler_params=pltpu.CompilerParams(vmem_limit_bytes=56 * 1024 * 1024),
         name="dress",

time: 148 us -> 147 us (level)
  no operation moved by 1% of the time
where the time goes in v3:
time: 147 us
  blocking collectives  141 us (96%)
  Pallas kernels  5.7 us (4%)
    all_to_all x1, blocking collectives, shards(): lax.all_to_all(send.reshape(owners, kinds, lanes), ('tens', 'rep'), 0, 0,...  84.2 us
    all_to_all x1, blocking collectives, shards(): partial = lax.all_to_all(partial, ('mat', 'rep'), 0, 0, tiled=True)  31.6 us
    all_to_all x1, blocking collectives, shards(): rows = lax.all_to_all(rows, 'tens', 0, 0, tiled=True)  25.4 us
    pallas_call x1, Pallas kernels, shards(): pl.pallas_call(dress_kernel, out_shape=jax.ShapeDtypeStruct((parts, cols...  4.03 us

profile of v3, /device:TPU:1, one launch (start us, length us, event | category | flops | bytes accessed | tf_op | source)
XLA Modules:
  0.0 146.9 jit_solution(14306110281855090222)
XLA Ops:
  0.0 4.0 %dress.1 = bf16[2,512,256]{2,1,0:T(8,128)(2,1)} custom-call(s32[4,4,4]{2,1,0:T(4,128)} %mask_hbm.1, bf16[64,512]{1,0:T(8,128)(2,1)} %bitcast.7, bf16[512,512]{1,0:T(8,128)(2,1)} %occ_hbm.1, bf16[4,512,512]{2,1,0:T(8,128)(2,1)} %slab_hbm.1), custom_call_target="tpu_custom_call" | custom-call | tf_op jit(solution)/shard_map/dress/pallas_call | solution.py:176
  4.0 84.2 %all_to_all.15 = bf16[128,8,256]{2,1,0:T(8,128)(2,1)S(1)} all-to-all(bf16[128,8,256]{2,1,0:T(8,128)(2,1)} %bitcast.6), channel_id=1, replica_groups=mesh['tens'=32,'mat'=8,'rep'=4] {'tens','rep'}, dimensions={0} | all-to-all | bytes 1048576 | tf_op jit(solution)/shard_map/all_to_all | solution.py:195
  88.2 0.7 pair.1
  89.0 31.6 %all_to_all.16.got_ref = bf16[32,64,128]{2,1,0:T(8,128)(2,1)S(1)} all-to-all(bf16[32,64,128]{2,1,0:T(8,128)(2,1)S(1)} %pair.1), channel_id=1, replica_groups=mesh['tens'=32,'mat'=8,'rep'=4] {'mat','rep'}, dimensions={0} | all-to-all | bytes 1048576 | tf_op jit(solution)/shard_map/all_to_all | solution.py:206
  120.5 0.3 plane_sum.1
  120.8 25.4 %all_to_all.17.got_ref = f32[32,2,128]{2,1,0:T(2,128)S(1)} all-to-all(f32[32,2,128]{2,1,0:T(2,128)S(1)} %bitcast.5), channel_id=1, replica_groups=mesh['tens'=32,'mat'=8,'rep'=4] {'tens'}, dimensions={0} | all-to-all | bytes 65536 | tf_op jit(solution)/shard_map/all_to_all | solution.py:215
  146.3 0.7 own_sum.1

commit v4 on v3

--- a/solution.py
+++ b/solution.py
@@ -18,8 +18,8 @@
 
 
 def dress_kernel(
-    mask_hbm, virt_hbm, occ_hbm, slab_hbm, out_hbm,
-    mask_ref, left_ref, occ_ref, slab_ref, half_ref, rows_ref, out_ref, sems,
+    mask_hbm, virt_hbm, occ_hbm, slab_hbm, out_ref,
+    mask_ref, left_ref, occ_ref, slab_ref, half_ref, rows_ref, sems,
 ):
     auxs, total, _ = slab_ref.shape
     blocks = mask_ref.shape[1]
@@ -31,7 +31,7 @@
     slabs = [
         pltpu.make_async_copy(slab_hbm.at[a], slab_ref.at[a], sems.at[3 + a]) for a in range(auxs)
     ]
-    for copy in [mask, virt] + slabs[:1] + [occ] + slabs[1:]:
+    for copy in [mask, virt] + slabs + [occ]:
         copy.start()
 
     start = lax.axis_index("mat") * cols
@@ -45,7 +45,6 @@
 
     mask.wait()
     virt.wait()
-    done = 0
     for a in range(auxs):
         slabs[a].wait()
         for b in range(0, blocks, 2):
@@ -61,17 +60,12 @@
             both = lax.dot_general(left_ref[...], strip, NT, preferred_element_type=F32).astype(BF)
             half_ref[a * cols : (a + 1) * cols, at] = both[:cols]
             rows_ref[(auxs + a) * cols : (auxs + a + 1) * cols, at] = both[cols:]
-        if a == 0:
-            occ.wait()
-        if a % 2 == 1 or a == auxs - 1:
-            at = slice(done * cols, (a + 1) * cols)
-            rows_ref[at, :] = jnp.dot(
-                half_ref[at, :], occ_ref[...], preferred_element_type=F32
-            ).astype(BF)
-            done = a + 1
+    occ.wait()
+    rows_ref[: auxs * cols, :] = jnp.dot(
+        half_ref[...], occ_ref[...], preferred_element_type=F32
+    ).astype(BF)
 
     parts, lanes = out_ref.shape[0], out_ref.shape[2]
-    outs = []
     for h in range(parts):
         for g in range(cols // band):
             rows = jnp.concatenate(
@@ -87,11 +81,6 @@
             out_ref[h, g * kinds * band : (g + 1) * kinds * band, :] = jnp.dot(
                 order, rows, preferred_element_type=F32
             ).astype(BF)
-        copy = pltpu.make_async_copy(out_ref.at[h], out_hbm.at[h], sems.at[3 + auxs + h])
-        copy.start()
-        outs.append(copy)
-    for copy in outs:
-        copy.wait()
 
 
 def pair_kernel(tens_count, rep_count, folds, scale, got_ref, out_ref):
@@ -177,7 +166,6 @@
         dress_kernel,
         out_shape=jax.ShapeDtypeStruct((parts, cols * kinds, lanes), BF),
         in_specs=[hbm] * 4,
-        out_specs=hbm,
         scratch_shapes=[
             pltpu.VMEM(block_mask.shape, jnp.int32),
             pltpu.VMEM((2 * cols, total), BF),
@@ -185,12 +173,16 @@
             pltpu.VMEM(integrals.shape, BF),
             pltpu.VMEM((auxs * cols, total), BF),
             pltpu.VMEM((kinds * cols, total), BF),
-            pltpu.VMEM((parts, cols * kinds, lanes), BF),
-            pltpu.SemaphoreType.DMA((3 + auxs + parts,)),
+            pltpu.SemaphoreType.DMA((3 + auxs,)),
         ],
-        compiler_params=pltpu.CompilerParams(vmem_limit_bytes=56 * 1024 * 1024),
+        compiler_params=LIMIT,
         name="dress",
-    )(block_mask, green_virt.T, green_occ, integrals)
+    )(
+        *[
+            pltpu.with_memory_space_constraint(x, pltpu.HBM)
+            for x in (block_mask, green_virt.T, green_occ, integrals)
+        ]
+    )
 
     got = lax.all_to_all(
         send.reshape(owners, kinds, lanes), ("tens", "rep"), 0, 0, tiled=True

time: 147 us -> 146 us (level)
  no operation moved by 1% of the time
where the time goes in v4:
time: 146 us
  blocking collectives  141 us (97%)
  Pallas kernels  4.99 us (3%)
    all_to_all x1, blocking collectives, shards(): lax.all_to_all(send.reshape(owners, kinds, lanes), ('tens', 'rep'), 0, 0,...  84 us
    all_to_all x1, blocking collectives, shards(): partial = lax.all_to_all(partial, ('mat', 'rep'), 0, 0, tiled=True)  31.6 us
    all_to_all x1, blocking collectives, shards(): rows = lax.all_to_all(rows, 'tens', 0, 0, tiled=True)  25.4 us
    pallas_call x1, Pallas kernels, shards(): pl.pallas_call(dress_kernel, out_shape=jax.ShapeDtypeStruct((parts, cols...  3.32 us

profile of v4, /device:TPU:1, one launch (start us, length us, event | category | flops | bytes accessed | tf_op | source)
XLA Modules:
  0.0 146.0 jit_solution(5314483723079332997)
XLA Ops:
  0.0 3.3 %dress.1 = bf16[2,512,256]{2,1,0:T(8,128)(2,1)S(1)} custom-call(s32[4,4,4]{2,1,0:T(4,128)} %mask_hbm.1, bf16[64,512]{1,0:T(8,128)(2,1)} %bitcast.7, bf16[512,512]{1,0:T(8,128)(2,1)} %occ_hbm.1, bf16[4,512,512]{2,1,0:T(8,128)(2,1)} %slab_hbm.1), custom_call_target="tpu_custom_call" | custom-call | tf_op jit(solution)/shard_map/dress/pallas_call | solution.py:165
  3.3 84.0 %all_to_all.15 = bf16[128,8,256]{2,1,0:T(8,128)(2,1)S(1)} all-to-all(bf16[128,8,256]{2,1,0:T(8,128)(2,1)S(1)} %bitcast.4), channel_id=1, replica_groups=mesh['tens'=32,'mat'=8,'rep'=4] {'tens','rep'}, dimensions={0} | all-to-all | bytes 1048576 | tf_op jit(solution)/shard_map/all_to_all | solution.py:187
  87.3 0.7 pair.1
  88.0 31.6 %all_to_all.16.got_ref = bf16[32,64,128]{2,1,0:T(8,128)(2,1)S(1)} all-to-all(bf16[32,64,128]{2,1,0:T(8,128)(2,1)S(1)} %pair.1), channel_id=1, replica_groups=mesh['tens'=32,'mat'=8,'rep'=4] {'mat','rep'}, dimensions={0} | all-to-all | bytes 1048576 | tf_op jit(solution)/shard_map/all_to_all | solution.py:198
  119.6 0.3 plane_sum.1
  119.9 25.4 %all_to_all.17.got_ref = f32[32,2,128]{2,1,0:T(2,128)S(1)} all-to-all(f32[32,2,128]{2,1,0:T(2,128)S(1)} %bitcast.6), channel_id=1, replica_groups=mesh['tens'=32,'mat'=8,'rep'=4] {'tens'}, dimensions={0} | all-to-all | bytes 65536 | tf_op jit(solution)/shard_map/all_to_all | solution.py:207
  145.3 0.7 own_sum.1

commit v5 on v4

--- a/solution.py
+++ b/solution.py
@@ -31,7 +31,7 @@
     slabs = [
         pltpu.make_async_copy(slab_hbm.at[a], slab_ref.at[a], sems.at[3 + a]) for a in range(auxs)
     ]
-    for copy in [mask, virt] + slabs + [occ]:
+    for copy in slabs[:1] + [mask, virt] + slabs[1:] + [occ]:
         copy.start()
 
     start = lax.axis_index("mat") * cols
@@ -44,17 +44,22 @@
     lane_block = lax.broadcasted_iota(jnp.int32, (1, total), 1) // width
 
     mask.wait()
+    factors = []
+    for a in range(auxs):
+        for row in range(blocks):
+            kept = mask_ref[a, row : row + 1, :].astype(F32)
+            factor = jnp.zeros((1, total), F32)
+            for c in range(blocks):
+                factor = jnp.where(lane_block == c, kept[:, c : c + 1], factor)
+            factors.append(factor.astype(BF))
     virt.wait()
     for a in range(auxs):
         slabs[a].wait()
         for b in range(0, blocks, 2):
             strips = []
             for row in (b, b + 1):
-                kept = mask_ref[a, row : row + 1, :].astype(F32)
-                factor = jnp.zeros((1, total), F32)
-                for c in range(blocks):
-                    factor = jnp.where(lane_block == c, kept[:, c : c + 1], factor)
-                strips.append(slab_ref[a, row * width : (row + 1) * width, :] * factor.astype(BF))
+                strip = slab_ref[a, row * width : (row + 1) * width, :]
+                strips.append(strip * factors[a * blocks + row])
             strip = jnp.concatenate(strips, axis=0)
             at = slice(b * width, (b + 2) * width)
             both = lax.dot_general(left_ref[...], strip, NT, preferred_element_type=F32).astype(BF)

time: 146 us -> 146 us (level)
  no operation moved by 1% of the time
where the time goes in v5:
time: 146 us
  blocking collectives  141 us (97%)
  Pallas kernels  4.61 us (3%)
    all_to_all x1, blocking collectives, shards(): lax.all_to_all(send.reshape(owners, kinds, lanes), ('tens', 'rep'), 0, 0,...  84 us
    all_to_all x1, blocking collectives, shards(): partial = lax.all_to_all(partial, ('mat', 'rep'), 0, 0, tiled=True)  31.6 us
    all_to_all x1, blocking collectives, shards(): rows = lax.all_to_all(rows, 'tens', 0, 0, tiled=True)  25.4 us
    pallas_call x1, Pallas kernels, shards(): pl.pallas_call(dress_kernel, out_shape=jax.ShapeDtypeStruct((parts, cols...  2.95 us

profile of v5, /device:TPU:1, one launch (start us, length us, event | category | flops | bytes accessed | tf_op | source)
XLA Modules:
  0.0 145.6 jit_solution(1154644550999004043)
XLA Ops:
  0.0 2.9 %dress.1 = bf16[2,512,256]{2,1,0:T(8,128)(2,1)S(1)} custom-call(s32[4,4,4]{2,1,0:T(4,128)} %mask_hbm.1, bf16[64,512]{1,0:T(8,128)(2,1)} %bitcast.7, bf16[512,512]{1,0:T(8,128)(2,1)} %occ_hbm.1, bf16[4,512,512]{2,1,0:T(8,128)(2,1)} %slab_hbm.1), custom_call_target="tpu_custom_call" | custom-call | tf_op jit(solution)/shard_map/dress/pallas_call | solution.py:170
  3.0 84.0 %all_to_all.15 = bf16[128,8,256]{2,1,0:T(8,128)(2,1)S(1)} all-to-all(bf16[128,8,256]{2,1,0:T(8,128)(2,1)S(1)} %bitcast.4), channel_id=1, replica_groups=mesh['tens'=32,'mat'=8,'rep'=4] {'tens','rep'}, dimensions={0} | all-to-all | bytes 1048576 | tf_op jit(solution)/shard_map/all_to_all | solution.py:192
  86.9 0.7 pair.1
  87.6 31.6 %all_to_all.16.got_ref = bf16[32,64,128]{2,1,0:T(8,128)(2,1)S(1)} all-to-all(bf16[32,64,128]{2,1,0:T(8,128)(2,1)S(1)} %pair.1), channel_id=1, replica_groups=mesh['tens'=32,'mat'=8,'rep'=4] {'mat','rep'}, dimensions={0} | all-to-all | bytes 1048576 | tf_op jit(solution)/shard_map/all_to_all | solution.py:203
  119.2 0.3 plane_sum.1
  119.5 25.4 %all_to_all.17.got_ref = f32[32,2,128]{2,1,0:T(2,128)S(1)} all-to-all(f32[32,2,128]{2,1,0:T(2,128)S(1)} %bitcast.6), channel_id=1, replica_groups=mesh['tens'=32,'mat'=8,'rep'=4] {'tens'}, dimensions={0} | all-to-all | bytes 65536 | tf_op jit(solution)/shard_map/all_to_all | solution.py:212
  145.0 0.7 own_sum.1

commit v6 on v5

--- a/solution.py
+++ b/solution.py
@@ -196,7 +196,7 @@
     folds = min(auxs, max(1, 128 // cols))
     partial = pl.pallas_call(
         lambda *refs: pair_kernel(tens_count, rep_count, folds, 1.0 / total, *refs),
-        out_shape=jax.ShapeDtypeStruct((mat_count * rep_count, cols, tens_count * auxs), BF),
+        out_shape=jax.ShapeDtypeStruct((mat_count * rep_count, cols, tens_count * auxs), F32),
         compiler_params=LIMIT,
         name="pair",
     )(got.reshape(owners * kinds, lanes))

time: 146 us -> 151 us (1.034)
  blocking collectives: 141 us -> 146 us
    all_to_all x1, blocking collectives: 31.6 us -> 36.2 us  [shards(): partial = lax.all_to_all(partial, ('mat', 'rep'), 0, 0, tiled=True)]
where the time goes in v6:
time: 151 us; the launch traced here: 150 us
  blocking collectives  146 us (97%)
  Pallas kernels  4.59 us (3%)
    all_to_all x1, blocking collectives, shards(): lax.all_to_all(send.reshape(owners, kinds, lanes), ('tens', 'rep'), 0, 0,...  84 us
    all_to_all x1, blocking collectives, shards(): partial = lax.all_to_all(partial, ('mat', 'rep'), 0, 0, tiled=True)  36.2 us
    all_to_all x1, blocking collectives, shards(): rows = lax.all_to_all(rows, 'tens', 0, 0, tiled=True)  25.4 us

profile of v6, /device:TPU:1, one launch (start us, length us, event | category | flops | bytes accessed | tf_op | source)
XLA Modules:
  0.0 150.2 jit_solution(8670775664667731984)
XLA Ops:
  0.0 2.9 %dress.1 = bf16[2,512,256]{2,1,0:T(8,128)(2,1)S(1)} custom-call(s32[4,4,4]{2,1,0:T(4,128)} %mask_hbm.1, bf16[64,512]{1,0:T(8,128)(2,1)} %bitcast.7, bf16[512,512]{1,0:T(8,128)(2,1)} %occ_hbm.1, bf16[4,512,512]{2,1,0:T(8,128)(2,1)} %slab_hbm.1), custom_call_target="tpu_custom_call" | custom-call | tf_op jit(solution)/shard_map/dress/pallas_call | solution.py:170
  3.0 84.0 %all_to_all.15 = bf16[128,8,256]{2,1,0:T(8,128)(2,1)S(1)} all-to-all(bf16[128,8,256]{2,1,0:T(8,128)(2,1)S(1)} %bitcast.5), channel_id=1, replica_groups=mesh['tens'=32,'mat'=8,'rep'=4] {'tens','rep'}, dimensions={0} | all-to-all | bytes 1048576 | tf_op jit(solution)/shard_map/all_to_all | solution.py:192
  86.9 0.7 pair.1
  87.6 36.2 %all_to_all.16.got_ref = f32[32,64,128]{2,1,0:T(8,128)S(1)} all-to-all(f32[32,64,128]{2,1,0:T(8,128)S(1)} %pair.1), channel_id=1, replica_groups=mesh['tens'=32,'mat'=8,'rep'=4] {'mat','rep'}, dimensions={0} | all-to-all | bytes 2097152 | tf_op jit(solution)/shard_map/all_to_all | solution.py:203
  123.9 0.3 plane_sum.1
  124.1 25.4 %all_to_all.17.got_ref = f32[32,2,128]{2,1,0:T(2,128)S(1)} all-to-all(f32[32,2,128]{2,1,0:T(2,128)S(1)} %bitcast.6), channel_id=1, replica_groups=mesh['tens'=32,'mat'=8,'rep'=4] {'tens'}, dimensions={0} | all-to-all | bytes 65536 | tf_op jit(solution)/shard_map/all_to_all | solution.py:212
  149.6 0.7 own_sum.1

commit v7 on v5

--- a/solution.py
+++ b/solution.py
@@ -123,15 +123,14 @@
         axis=0,
     )
     slots, cols, lanes = out_ref.shape
-    for g, group in enumerate(groups):
-        block = lax.dot_general(group[rows // 2 :], dressed, NT, preferred_element_type=F32)
-        block = (block * scale).astype(out_ref.dtype)
-        per = block.shape[0] // cols
-        for k in range(per):
-            for r in range(rep_count):
-                out_ref[(g * per + k) * rep_count + r] = block[
-                    k * cols : (k + 1) * cols, r * lanes : (r + 1) * lanes
-                ]
+    masked = jnp.concatenate([group[rows // 2 :] for group in groups], axis=0)
+    block = lax.dot_general(masked, dressed, NT, preferred_element_type=F32)
+    block = (block * scale).astype(out_ref.dtype)
+    for k in range(slots // rep_count):
+        for r in range(rep_count):
+            out_ref[k * rep_count + r] = block[
+                k * cols : (k + 1) * cols, r * lanes : (r + 1) * lanes
+            ]
 
 
 def plane_kernel(got_ref, out_ref):

time: 146 us -> 146 us (level)
  no operation moved by 1% of the time
where the time goes in v7:
time: 146 us
  blocking collectives  141 us (97%)
  Pallas kernels  4.49 us (3%)
    all_to_all x1, blocking collectives, shards(): lax.all_to_all(send.reshape(owners, kinds, lanes), ('tens', 'rep'), 0, 0,...  84 us
    all_to_all x1, blocking collectives, shards(): partial = lax.all_to_all(partial, ('mat', 'rep'), 0, 0, tiled=True)  31.6 us
    all_to_all x1, blocking collectives, shards(): rows = lax.all_to_all(rows, 'tens', 0, 0, tiled=True)  25.4 us
    pallas_call x1, Pallas kernels, shards(): pl.pallas_call(dress_kernel, out_shape=jax.ShapeDtypeStruct((parts, cols...  2.95 us

profile of v7, /device:TPU:1, one launch (start us, length us, event | category | flops | bytes accessed | tf_op | source)
XLA Modules:
  0.0 145.5 jit_solution(15500298030403080911)
XLA Ops:
  0.0 2.9 %dress.1 = bf16[2,512,256]{2,1,0:T(8,128)(2,1)S(1)} custom-call(s32[4,4,4]{2,1,0:T(4,128)} %mask_hbm.1, bf16[64,512]{1,0:T(8,128)(2,1)} %bitcast.7, bf16[512,512]{1,0:T(8,128)(2,1)} %occ_hbm.1, bf16[4,512,512]{2,1,0:T(8,128)(2,1)} %slab_hbm.1), custom_call_target="tpu_custom_call" | custom-call | tf_op jit(solution)/shard_map/dress/pallas_call | solution.py:169
  3.0 84.0 %all_to_all.15 = bf16[128,8,256]{2,1,0:T(8,128)(2,1)S(1)} all-to-all(bf16[128,8,256]{2,1,0:T(8,128)(2,1)S(1)} %bitcast.4), channel_id=1, replica_groups=mesh['tens'=32,'mat'=8,'rep'=4] {'tens','rep'}, dimensions={0} | all-to-all | bytes 1048576 | tf_op jit(solution)/shard_map/all_to_all | solution.py:191
  86.9 0.6 pair.1
  87.5 31.6 %all_to_all.16.got_ref = bf16[32,64,128]{2,1,0:T(8,128)(2,1)S(1)} all-to-all(bf16[32,64,128]{2,1,0:T(8,128)(2,1)S(1)} %pair.1), channel_id=1, replica_groups=mesh['tens'=32,'mat'=8,'rep'=4] {'mat','rep'}, dimensions={0} | all-to-all | bytes 1048576 | tf_op jit(solution)/shard_map/all_to_all | solution.py:202
  119.1 0.3 plane_sum.1
  119.4 25.4 %all_to_all.17.got_ref = f32[32,2,128]{2,1,0:T(2,128)S(1)} all-to-all(f32[32,2,128]{2,1,0:T(2,128)S(1)} %bitcast.6), channel_id=1, replica_groups=mesh['tens'=32,'mat'=8,'rep'=4] {'tens'}, dimensions={0} | all-to-all | bytes 65536 | tf_op jit(solution)/shard_map/all_to_all | solution.py:211
  144.8 0.7 own_sum.1

commit v8 on v7

--- a/solution.py
+++ b/solution.py
@@ -66,12 +66,12 @@
             half_ref[a * cols : (a + 1) * cols, at] = both[:cols]
             rows_ref[(auxs + a) * cols : (auxs + a + 1) * cols, at] = both[cols:]
     occ.wait()
-    rows_ref[: auxs * cols, :] = jnp.dot(
-        half_ref[...], occ_ref[...], preferred_element_type=F32
-    ).astype(BF)
-
     parts, lanes = out_ref.shape[0], out_ref.shape[2]
     for h in range(parts):
+        at = slice(h * lanes, (h + 1) * lanes)
+        rows_ref[: auxs * cols, at] = jnp.dot(
+            half_ref[...], occ_ref[:, at], preferred_element_type=F32
+        ).astype(BF)
         for g in range(cols // band):
             rows = jnp.concatenate(
                 [

time: 146 us -> 146 us (level)
  no operation moved by 1% of the time
where the time goes in v8:
time: 146 us
  blocking collectives  141 us (97%)
  Pallas kernels  4.57 us (3%)
    all_to_all x1, blocking collectives, shards(): lax.all_to_all(send.reshape(owners, kinds, lanes), ('tens', 'rep'), 0, 0,...  84 us
    all_to_all x1, blocking collectives, shards(): partial = lax.all_to_all(partial, ('mat', 'rep'), 0, 0, tiled=True)  31.6 us
    all_to_all x1, blocking collectives, shards(): rows = lax.all_to_all(rows, 'tens', 0, 0, tiled=True)  25.4 us
    pallas_call x1, Pallas kernels, shards(): pl.pallas_call(dress_kernel, out_shape=jax.ShapeDtypeStruct((parts, cols...  3.04 us

profile of v8, /device:TPU:1, one launch (start us, length us, event | category | flops | bytes accessed | tf_op | source)
XLA Modules:
  0.0 145.6 jit_solution(14315384423666258085)
XLA Ops:
  0.0 3.0 %dress.1 = bf16[2,512,256]{2,1,0:T(8,128)(2,1)S(1)} custom-call(s32[4,4,4]{2,1,0:T(4,128)} %mask_hbm.1, bf16[64,512]{1,0:T(8,128)(2,1)} %bitcast.7, bf16[512,512]{1,0:T(8,128)(2,1)} %occ_hbm.1, bf16[4,512,512]{2,1,0:T(8,128)(2,1)} %slab_hbm.1), custom_call_target="tpu_custom_call" | custom-call | tf_op jit(solution)/shard_map/dress/pallas_call | solution.py:169
  3.0 84.0 %all_to_all.15 = bf16[128,8,256]{2,1,0:T(8,128)(2,1)S(1)} all-to-all(bf16[128,8,256]{2,1,0:T(8,128)(2,1)S(1)} %bitcast.4), channel_id=1, replica_groups=mesh['tens'=32,'mat'=8,'rep'=4] {'tens','rep'}, dimensions={0} | all-to-all | bytes 1048576 | tf_op jit(solution)/shard_map/all_to_all | solution.py:191
  87.0 0.6 pair.1
  87.6 31.6 %all_to_all.16.got_ref = bf16[32,64,128]{2,1,0:T(8,128)(2,1)S(1)} all-to-all(bf16[32,64,128]{2,1,0:T(8,128)(2,1)S(1)} %pair.1), channel_id=1, replica_groups=mesh['tens'=32,'mat'=8,'rep'=4] {'mat','rep'}, dimensions={0} | all-to-all | bytes 1048576 | tf_op jit(solution)/shard_map/all_to_all | solution.py:202
  119.2 0.3 plane_sum.1
  119.5 25.4 %all_to_all.17.got_ref = f32[32,2,128]{2,1,0:T(2,128)S(1)} all-to-all(f32[32,2,128]{2,1,0:T(2,128)S(1)} %bitcast.6), channel_id=1, replica_groups=mesh['tens'=32,'mat'=8,'rep'=4] {'tens'}, dimensions={0} | all-to-all | bytes 65536 | tf_op jit(solution)/shard_map/all_to_all | solution.py:211
  144.9 0.7 own_sum.1

commit v9 on v5

--- a/solution.py
+++ b/solution.py
@@ -37,7 +37,7 @@
     start = lax.axis_index("mat") * cols
     left_ref[cols:, :] = one_hot(cols, total, lambda row: row + start)
     kinds = rows_ref.shape[0] // cols
-    band = min(cols, 32)
+    band = min(cols, 16)
     order = one_hot(
         kinds * band, kinds * band, lambda row: (row % kinds) * band + row // kinds
     )

time: 146 us -> 146 us (level)
  no operation moved by 1% of the time
where the time goes in v9:
time: 146 us
  blocking collectives  141 us (97%)
  Pallas kernels  4.6 us (3%)
    all_to_all x1, blocking collectives, shards(): lax.all_to_all(send.reshape(owners, kinds, lanes), ('tens', 'rep'), 0, 0,...  84 us
    all_to_all x1, blocking collectives, shards(): partial = lax.all_to_all(partial, ('mat', 'rep'), 0, 0, tiled=True)  31.6 us
    all_to_all x1, blocking collectives, shards(): rows = lax.all_to_all(rows, 'tens', 0, 0, tiled=True)  25.4 us
    pallas_call x1, Pallas kernels, shards(): pl.pallas_call(dress_kernel, out_shape=jax.ShapeDtypeStruct((parts, cols...  2.93 us

profile of v9, /device:TPU:1, one launch (start us, length us, event | category | flops | bytes accessed | tf_op | source)
XLA Modules:
  0.0 145.6 jit_solution(5883626335894007696)
XLA Ops:
  0.0 2.9 %dress.1 = bf16[2,512,256]{2,1,0:T(8,128)(2,1)S(1)} custom-call(s32[4,4,4]{2,1,0:T(4,128)} %mask_hbm.1, bf16[64,512]{1,0:T(8,128)(2,1)} %bitcast.7, bf16[512,512]{1,0:T(8,128)(2,1)} %occ_hbm.1, bf16[4,512,512]{2,1,0:T(8,128)(2,1)} %slab_hbm.1), custom_call_target="tpu_custom_call" | custom-call | tf_op jit(solution)/shard_map/dress/pallas_call | solution.py:170
  2.9 84.0 %all_to_all.15 = bf16[128,8,256]{2,1,0:T(8,128)(2,1)S(1)} all-to-all(bf16[128,8,256]{2,1,0:T(8,128)(2,1)S(1)} %bitcast.4), channel_id=1, replica_groups=mesh['tens'=32,'mat'=8,'rep'=4] {'tens','rep'}, dimensions={0} | all-to-all | bytes 1048576 | tf_op jit(solution)/shard_map/all_to_all | solution.py:192
  86.9 0.7 pair.1
  87.6 31.6 %all_to_all.16.got_ref = bf16[32,64,128]{2,1,0:T(8,128)(2,1)S(1)} all-to-all(bf16[32,64,128]{2,1,0:T(8,128)(2,1)S(1)} %pair.1), channel_id=1, replica_groups=mesh['tens'=32,'mat'=8,'rep'=4] {'mat','rep'}, dimensions={0} | all-to-all | bytes 1048576 | tf_op jit(solution)/shard_map/all_to_all | solution.py:203
  119.2 0.3 plane_sum.1
  119.5 25.4 %all_to_all.17.got_ref = f32[32,2,128]{2,1,0:T(2,128)S(1)} all-to-all(f32[32,2,128]{2,1,0:T(2,128)S(1)} %bitcast.6), channel_id=1, replica_groups=mesh['tens'=32,'mat'=8,'rep'=4] {'tens'}, dimensions={0} | all-to-all | bytes 65536 | tf_op jit(solution)/shard_map/all_to_all | solution.py:212
  144.9 0.7 own_sum.1
